TPU v7x, 256 devices: a whole 4x4x8 slice. The times are simulated.
256 devices in a mesh: gx: 4 (over x), gy: 8 (over z_hi, core), gz: 8 (over z_lo, y).
Axes of the slice: x: 4, y: 4, z: 8 (z_hi: 4, z_lo: 2; z = z_hi * 2 + z_lo), core: 2. Of those that a mesh axis runs over, the one named last changes fastest.
Arguments:
- latent: float32 [3, 64, 128, 512], P(None, 'gy', 'gz', 'gx'), may hold values from -6 to 6
- cotangent: float32 [3, 64, 128, 512], P(None, 'gy', 'gz', 'gx'), may hold values from -6 to 6
Outputs:
- moved: float32 [3, 64, 128, 512], P(None, 'gy', 'gz', 'gx')
- grad_latent: float32 [3, 64, 128, 512], P(None, 'gy', 'gz', 'gx')
All inputs are finite; a program needn't handle non-finite values.
Results may differ from a plain program's by a relative error of at most 0.0003.
Values sent between devices are 32-bit elements; how exact they have to be, the bound alone decides.
A program may use at most 128 MiB of HBM per device.

v0:
```python
import functools
import math

import jax
import jax.numpy as jnp
import numpy as np
from jax import lax
from jax.experimental import pallas as pl
from jax.experimental.pallas import tpu as pltpu
from jax.sharding import PartitionSpec as P

SMAX = 0.45
STEP = 0.5
SHORT = 4.0
COUPLE = 0.5
SPREAD = 0.125
KERNEL = (0.05, 0.25, 0.4, 0.25, 0.05)
MESH = pl.DeviceIdType.MESH

BX, BY, BZ = 8, 16, 128
CX, CY, CZ = 4, 8, 64
WX, WY = 16, 24


def basis(length):
    n = np.arange(length)
    angle = 2.0 * np.pi * ((n[:, None] * n[None, :]) % length) / length
    return (np.cos(angle) + np.sin(angle)) / math.sqrt(length)


def five(delta):
    return np.where(np.abs(delta) <= 2, np.take(np.array(KERNEL), np.clip(delta + 2, 0, 4)), 0.0)


def same(left, right):
    return (left[:, None] == right[None, :]).astype(np.float64)


def central(left, right):
    return 0.5 * (same(left + 1, right) - same(left - 1, right))


def make_tables(ngx, ngy, ngz):
    mx, my, mz = CX * ngy, CY * ngz, CZ * ngx
    qx, qy, qz = basis(mx), basis(my), basis(mz)
    f = {}
    cxe, cye = np.arange(-1, CX + 1), np.arange(-1, CY + 1)
    fx, fy = np.arange(-1, BX + 1), np.arange(-4, BY + 4)
    ox, oy, oz = np.arange(BX), np.arange(BY), np.arange(BZ)
    down = lambda v: np.floor_divide(v, 2)

    def rows64(matrix):
        return np.concatenate([matrix, np.zeros((64 - matrix.shape[0], matrix.shape[1]))])

    f["cd"] = rows64(np.kron(same(cxe, down(fx)), same(cye, down(fy)) * ((fy >= -1) & (fy <= BY))))
    own_x, own_y = same(cxe, down(ox)), same(cye, down(oy))
    f["cp"] = rows64(
        np.concatenate(
            [
                np.kron(-central(cxe, down(ox)), own_y),
                np.kron(own_x, -central(cye, down(oy))),
                np.kron(own_x, own_y),
            ],
            axis=1,
        )
    )
    zt = np.zeros((ngx, 512, ngx, 2, CZ))
    for c in range(ngx):
        zc = CZ * c + down(oz)
        q = qz.reshape(mz, ngx, CZ)
        zt[c, 0:128, :, 0] = q[zc % mz]
        zt[c, 128, :, 0] = q[(CZ * c + CZ) % mz]
        zt[c, 255, :, 0] = q[(CZ * c - 1) % mz]
        zt[c, 256:384, :, 1] = q[zc % mz]
        zt[c, 384:512, :, 1] = 0.5 * (q[(zc + 1) % mz] - q[(zc - 1) % mz])
    f["zt"] = zt.reshape(ngx, 512, ngx * 128)
    yt = np.zeros((ngz, ngz, 6, CY, 64))
    for b in range(ngz):
        for x in range(6):
            for y in range(10):
                yt[b, :, x, :, x * 10 + y] = qy[(CY * b + y - 1) % my].reshape(ngz, CY)
    f["yt"] = yt.reshape(ngz, ngz * 48, 64)
    xf = np.zeros((mx, CY, ngy, 6, CY))
    xi = np.zeros((ngy, 6, CY, mx, CY))
    for a in range(ngy):
        for x in range(6):
            for m in range(CY):
                xf[:, m, a, x, m] = qx[(CX * a + x - 1) % mx]
                xi[a, x, m, :, m] = qx[(CX * a + x - 1) % mx]
    f["xf"] = xf.reshape(mx * CY, ngy * 48)
    f["xi"] = xi.reshape(ngy, 48, mx * CY)
    square = lambda total: 4.0 * np.sin(np.pi * np.arange(total) / total) ** 2
    ka = square(mx)[None, :, None] + square(my).reshape(ngz, 1, CY)
    f["ka"] = np.broadcast_to(ka.reshape(ngz, mx * CY, 1), (ngz, mx * CY, 128))
    kb = np.concatenate([square(mz).reshape(ngx, CZ)] * 2, axis=1)
    f["kb"] = np.broadcast_to(kb[:, None], (ngx, 8, 128))
    yi = np.zeros((ngz, 64, ngz, 6, CY))
    for b in range(ngz):
        for x in range(6):
            for y in range(10):
                yi[b, x * 10 + y, :, x, :] = qy[(CY * b + y - 1) % my].reshape(ngz, CY)
    f["yi"] = yi.reshape(ngz, 64, ngz * 48)
    zi = np.zeros((ngx, ngx, 2, CZ, 640))
    for c in range(ngx):
        at = lambda cell: qz[(CZ * c + cell) % mz].T.reshape(ngx, CZ, 128)
        zi[c, :, 0, :, 0:128] = at(down(oz))
        zi[c, :, 0, :, 128:256] = 0.5 * (at(down(oz) + 1) - at(down(oz) - 1))
        for k in range(3):
            zi[c, :, 1, :, 256 + 128 * k : 384 + 128 * k] = at(down(oz + k - 1))
    f["zi"] = zi.reshape(ngx, ngx * 128, 640)
    pad4 = lambda matrix: np.concatenate([matrix, np.zeros((matrix.shape[0], 4))], axis=1)
    f["uf"] = np.stack(
        [
            pad4(np.kron(central(down(ox), cxe), same(down(oy), cye))),
            pad4(np.kron(same(down(ox), cxe), central(down(oy), cye))),
            pad4(np.kron(same(down(ox), cxe), same(down(oy), cye))),
        ]
    )
    ry = np.arange(-1, WY - 1)
    row = ((ry <= BY) * 1.0)[:, None]
    f["up"] = pad4(np.kron(same(down(fx), cxe), same(down(ry), cye) * row))
    zw = np.concatenate([oz, oz + 128])
    zw[252:256] = np.arange(-4, 0)
    valid = np.concatenate([np.ones(128), np.ones(4), np.zeros(120), np.ones(4)])[:, None]
    tap = lambda target, extra: five(target[None, :] + extra - zw[:, None]) * valid
    f["sz"] = np.concatenate(
        [tap(oz + k, 0) for k in (-1, 0, 1)]
        + [tap(oz + k, 1) - tap(oz + k, -1) for k in (-1, 0, 1)],
        axis=1,
    )
    wx, wy = np.arange(-4, WX - 4), np.arange(-4, WY - 4)
    kx = lambda extra: five(fx[:, None] + extra - wx[None, :])
    ky = lambda extra: five(ry[:, None] + extra - wy[None, :]) * row
    half = 0.5 * SHORT
    f["an"] = np.stack(
        [
            half * np.kron(kx(1) - kx(-1), ky(0)),
            half * np.kron(kx(0), ky(1) - ky(-1)),
            half * np.kron(kx(0), ky(0)),
        ]
    )
    return {name: np.ascontiguousarray(value, dtype=np.float32) for name, value in f.items()}


def dot(left, right):
    return jnp.dot(
        left, right, precision=lax.Precision.HIGHEST, preferred_element_type=jnp.float32
    )


NAMES = ("cd", "cp", "zt", "yt", "xf", "xi", "ka", "kb", "yi", "zi", "uf", "up", "sz", "an")
AXIS_OF = {"zt": "gx", "yt": "gz", "xi": "gy", "ka": "gz", "kb": "gx", "yi": "gz", "zi": "gx"}


def kernel(sizes, lat, cot, *refs):
    ngx, ngy, ngz = sizes
    tables = dict(zip(NAMES, refs[: len(NAMES)]))
    moved, grad = refs[len(NAMES) : len(NAMES) + 2]
    rest = refs[len(NAMES) + 2 :]
    local = dict(zip(NAMES, rest[: len(NAMES)]))
    (
        bent, wt, vals, bk, f0, t1, hp, tsend, trecv, yrecv, yhrecv, xrecv, xhrecv,
        zbuf, zrecv, ybuf, yrec, xrec, urec, wrec, near, psi, part,
        table_sem, s_z, r_z, s_y, r_y, s_u, r_u, s_w, r_w, s_x, r_x, s_h, r_h,
    ) = rest[len(NAMES) :]
    c, a, b = lax.axis_index("gx"), lax.axis_index("gy"), lax.axis_index("gz")
    place = {"gx": c, "gy": a, "gz": b}
    size = {"gx": ngx, "gy": ngy, "gz": ngz}

    loads = {}
    for number, name in enumerate(NAMES):
        source = tables[name]
        if name in AXIS_OF:
            source = source.at[place[AXIS_OF[name]]]
        loads[name] = pltpu.make_async_copy(source, local[name], table_sem.at[number])
        loads[name].start()

    def other(axis, step):
        return {axis: lax.rem(place[axis] + step, size[axis])}

    barrier = pltpu.get_barrier_semaphore()
    partners = [(axis, step) for axis in size for step in range(1, size[axis])]
    for axis, step in partners:
        pl.semaphore_signal(barrier, inc=1, device_id=other(axis, step), device_id_type=MESH)

    started = []

    def send(source, target, send_sem, recv_sem, axis, step):
        copy = pltpu.make_async_remote_copy(
            src_ref=source,
            dst_ref=target,
            send_sem=send_sem,
            recv_sem=recv_sem,
            device_id=other(axis, step),
            device_id_type=MESH,
        )
        copy.start()
        return copy

    lane = lax.broadcasted_iota(jnp.int32, (WY, 128), 1)
    edge = jnp.logical_or(lane < 4, lane >= 124)
    upper = lax.rem(lane, 8) >= 4

    wt[...] = jnp.zeros_like(wt)
    f0[...] = jnp.zeros_like(f0)
    t1[...] = jnp.zeros_like(t1)
    hp[...] = jnp.zeros_like(hp)
    vals[...] = jnp.zeros_like(vals)
    bk[...] = jnp.zeros_like(bk)
    for axis in range(3):
        bend = jnp.tanh(lat[axis])
        bent[axis] = bend
        shift = SMAX * bend
        wt[3 * axis, 2:10, 8:24] = 0.5 * (0.5 - shift) ** 2
        wt[3 * axis + 1, 2:10, 8:24] = 0.75 - shift * shift
        wt[3 * axis + 2, 2:10, 8:24] = 0.5 * (0.5 + shift) ** 2
        vals[axis, 2:10, 8:24] = STEP * cot[axis]

    def gathered(plane, charges):
        totals = [[None] * 3 for _ in range(charges or 1)]
        for i in range(3):
            at = plane + 2 - i
            for j in range(3):
                rows = pl.ds(5 - j, WY)
                cross = wt[i, at, rows, :] * wt[3 + j, at, rows, :]
                for k in range(3):
                    weight = cross * wt[6 + k, at, rows, :]
                    for q in range(charges or 1):
                        term = weight * vals[q, at, rows, :] if charges else weight
                        totals[q][k] = term if totals[q][k] is None else totals[q][k] + term
        return totals

    def paint(plane, carry):
        ((low, middle, high),) = gathered(plane, 0)
        low = pltpu.roll(low, 127, 1)
        high = pltpu.roll(high, 1, 1)
        keep_low, keep_high = lane < 127, lane >= 1
        main = middle + jnp.where(keep_low, low, 0.0) + jnp.where(keep_high, high, 0.0)
        spill = jnp.where(keep_low, 0.0, low) + jnp.where(keep_high, 0.0, high)
        f0[0, plane + 3] = main
        t1[0, plane + 3] = spill
        return carry

    lax.fori_loop(0, BX + 2, paint, 0)

    loads["cd"].wait()
    loads["cp"].wait()
    inner = BX + 2
    density = jnp.concatenate(
        [f0[0, 3:13].reshape(inner * WY, 128), t1[0, 3:13].reshape(inner * WY, 128)], axis=1
    )
    rho = dot(local["cd"][...], density)
    pushed = [(STEP * cot[axis]).reshape(BX * BY, 128) for axis in range(3)]
    cross_source = dot(local["cp"][:, 0:256], jnp.concatenate(pushed[:2], axis=0))
    along_source = dot(local["cp"][:, 256:384], pushed[2])
    loads["zt"].wait()
    modes = dot(jnp.concatenate([rho, cross_source, along_source], axis=1), local["zt"][...])
    for j in range(ngx):
        zbuf[j] = modes[:, 128 * j : 128 * (j + 1)]
    pl.semaphore_wait(barrier, len(partners))
    z_copies = [
        send(zbuf.at[lax.rem(c + d, ngx)], zrecv.at[d], s_z.at[d], r_z.at[d], "gx", d)
        for d in range(1, ngx)
    ]
    started += z_copies

    def paint_back(plane, carry):
        totals = gathered(plane, 3)
        for q in range(3):
            for k in range(3):
                bk[3 * q + k, plane + 2, 8:32, :] = totals[q][k]
        return carry

    lax.fori_loop(0, BX + 2, paint_back, 0)

    def spread_back(plane, carry):
        at = plane + 1

        def cross(k):
            return 0.5 * (
                bk[k, at + 1, 8:32, :] - bk[k, at - 1, 8:32, :]
                + bk[3 + k, at, 9:33, :] - bk[3 + k, at, 7:31, :]
            )

        up = [0.5 * bk[6 + k, at, 8:32, :] for k in range(3)]
        parts = {
            -2: up[0],
            -1: cross(0) + up[1],
            1: cross(2) - up[1],
            2: -up[2],
        }
        main = cross(1) + up[2] - up[0]
        spill = None
        for step, value in parts.items():
            rolled = pltpu.roll(value, step % 128, 1)
            keep = lane >= step if step > 0 else lane < 128 + step
            main = main + jnp.where(keep, rolled, 0.0)
            over = jnp.where(keep, 0.0, rolled)
            spill = over if spill is None else spill + over
        f0[1, plane + 2] = main
        t1[1, plane + 2] = spill
        return carry

    lax.fori_loop(0, BX + 4, spread_back, 0)

    def pack(plane, carry):
        by = 8 * plane + 4
        out = []
        for q in range(2):
            out.append(carry[2 * q] + pltpu.roll(jnp.where(edge, f0[q, plane], 0.0), by, 1))
            out.append(carry[2 * q + 1] + pltpu.roll(t1[q, plane], by, 1))
        return tuple(out)

    empty = jnp.zeros((WY, 128), jnp.float32)
    packed = lax.fori_loop(2, BX + 6, pack, (empty,) * 4)
    for q in range(2):
        face, spill = packed[2 * q], packed[2 * q + 1]
        tsend[0, q] = jnp.where(upper, spill, face)
        tsend[1, q] = jnp.where(upper, face, spill)
        hp[q] = spill
    t_copies = [
        send(tsend.at[0], trecv.at[0], s_h.at[0], r_h.at[0], "gx", 1),
        send(tsend.at[1], trecv.at[1], s_h.at[1], r_h.at[1], "gx", ngx - 1),
    ]
    started += t_copies

    for copy in z_copies:
        copy.wait_recv()
    total = zbuf[c]
    for d in range(1, ngx):
        total = total + zrecv[d]
    loads["yt"].wait()
    ybuf[...] = dot(local["yt"][...], total).reshape(ngz, 48, 128)
    y_copies = [
        send(ybuf.at[lax.rem(b + d, ngz)], yrec.at[d], s_y.at[d], r_y.at[d], "gz", d)
        for d in range(1, ngz)
    ]
    started += y_copies

    for copy in t_copies:
        copy.wait_recv()
    fixes = []
    for q in range(2):
        from_left, from_right = trecv[0, q], trecv[1, q]
        hp[q] = hp[q] + jnp.where(upper, from_right, from_left)
        fixes.append(jnp.where(upper, from_left, from_right))

    def fix(plane, carry):
        by = 124 - 8 * plane
        by = jnp.where(by < 0, by + 128, by)
        for q in range(2):
            f0[q, plane] = f0[q, plane] + jnp.where(edge, pltpu.roll(fixes[q], by, 1), 0.0)
        return carry

    lax.fori_loop(2, BX + 6, fix, 0)
    rim_copies = [
        send(f0.at[:, 2:14, 16:24], yrecv.at[0], s_h.at[2], r_h.at[2], "gz", 1),
        send(f0.at[:, 2:14, 0:8], yrecv.at[1], s_h.at[3], r_h.at[3], "gz", ngz - 1),
        send(hp.at[:, 16:24], yhrecv.at[0], s_h.at[4], r_h.at[4], "gz", 1),
        send(hp.at[:, 0:8], yhrecv.at[1], s_h.at[5], r_h.at[5], "gz", ngz - 1),
    ]

    for copy in y_copies:
        copy.wait_recv()
    total = ybuf[b]
    for d in range(1, ngz):
        total = total + yrec[d]
    xrec[a] = total
    x_copies = [
        send(xrec.at[a], xrec.at[a], s_x.at[d], r_x.at[d], "gy", d) for d in range(1, ngy)
    ]
    started += x_copies

    for copy in rim_copies:
        copy.wait()
    f0[:, 2:14, 0:8] = f0[:, 2:14, 0:8] + yrecv[0]
    f0[:, 2:14, 16:24] = f0[:, 2:14, 16:24] + yrecv[1]
    hp[:, 0:8] = hp[:, 0:8] + yhrecv[0]
    hp[:, 16:24] = hp[:, 16:24] + yhrecv[1]
    side_copies = [
        send(f0.at[0, 8:13], xrecv.at[0, 0], s_h.at[6], r_h.at[6], "gy", 1),
        send(f0.at[1, 9:14], xrecv.at[0, 1], s_h.at[7], r_h.at[7], "gy", 1),
        send(f0.at[0, 3:8], xrecv.at[1, 0], s_h.at[8], r_h.at[8], "gy", ngy - 1),
        send(f0.at[1, 2:7], xrecv.at[1, 1], s_h.at[9], r_h.at[9], "gy", ngy - 1),
        send(hp, xhrecv.at[0], s_h.at[10], r_h.at[10], "gy", 1),
        send(hp, xhrecv.at[1], s_h.at[11], r_h.at[11], "gy", ngy - 1),
    ]

    loads["ka"].wait()
    loads["kb"].wait()
    squares = local["ka"][...] + local["kb"][0:1, :]
    zero = squares == 0.0
    gain = jnp.where(
        zero, 0.0, COUPLE * jnp.exp(-SPREAD * squares) / jnp.where(zero, 1.0, squares)
    )
    loads["xf"].wait()
    loads["xi"].wait()
    for copy in x_copies:
        copy.wait_recv()
    spectrum = dot(local["xf"][...], xrec[...].reshape(ngy * 48, 128))
    urec[b] = dot(local["xi"][...], gain * spectrum)
    u_copies = [
        send(urec.at[b], urec.at[b], s_u.at[d], r_u.at[d], "gz", d) for d in range(1, ngz)
    ]
    started += u_copies

    for copy in side_copies:
        copy.wait()
    f0[0, 0:5] = f0[0, 0:5] + xrecv[0, 0]
    f0[1, 1:6] = f0[1, 1:6] + xrecv[0, 1]
    f0[0, 11:16] = f0[0, 11:16] + xrecv[1, 0]
    f0[1, 10:15] = f0[1, 10:15] + xrecv[1, 1]
    rims = [
        hp[q]
        + jnp.where(
            lane < 64, pltpu.roll(xhrecv[0, q], 64, 1), pltpu.roll(xhrecv[1, q], 64, 1)
        )
        for q in range(2)
    ]

    def unpack(plane, carry):
        by = 124 - 8 * plane
        by = jnp.where(by < 0, by + 128, by)
        for q in range(2):
            t1[q, plane] = jnp.where(edge, pltpu.roll(rims[q], by, 1), 0.0)
        return carry

    lax.fori_loop(0, WX, unpack, 0)
    window = [
        jnp.concatenate([f0[q].reshape(WX * WY, 128), t1[q].reshape(WX * WY, 128)], axis=1)
        for q in range(2)
    ]
    loads["sz"].wait()
    loads["an"].wait()

    def keep(target, slot, value):
        for k in range(3):
            target[slot, k] = value[:, 128 * k : 128 * (k + 1)].reshape(inner, WY, 128)

    smoothed = dot(window[0], local["sz"][:, 0:384])
    keep(near, 0, dot(local["an"][0], smoothed))
    keep(near, 1, dot(local["an"][1], smoothed))
    keep(near, 2, dot(local["an"][2], dot(window[0], local["sz"][:, 384:768])))
    keep(near, 3, -2.0 * dot(local["an"][2], dot(window[1], local["sz"][:, 0:384])))

    loads["yi"].wait()
    for copy in u_copies:
        copy.wait_recv()
    wrec[c] = dot(local["yi"][...], urec[...].reshape(ngz * 48, 128))
    w_copies = [
        send(wrec.at[c], wrec.at[c], s_w.at[d], r_w.at[d], "gx", d) for d in range(1, ngx)
    ]
    started += w_copies

    def slopes(plane):
        rows = pl.ds(8, BY)
        weights = [wt[n, plane + 2, rows, :] for n in range(9)]
        slope = []
        for axis in range(3):
            shift = SMAX * bent[axis, plane]
            slope += [shift - 0.5, -2.0 * shift, shift + 0.5]
        return weights, slope

    def plus(total, term):
        return term if total is None else total + term

    def read(plane, carry):
        weights, slope = slopes(plane)
        pushes = [vals[axis, plane + 2, 8:24, :] for axis in range(3)]
        sums = [None] * 6
        for k in range(3):
            mid = [None] * 6
            for j in range(3):
                line = [None] * 5
                for i in range(3):
                    at = [near[q, k, plane + i, pl.ds(j, BY), :] for q in range(4)]
                    both = at[3]
                    for q in range(3):
                        line[q] = plus(line[q], weights[i] * at[q])
                        both = both + pushes[q] * at[q]
                    line[3] = plus(line[3], weights[i] * both)
                    line[4] = plus(line[4], slope[i] * both)
                for q in range(3):
                    mid[q] = plus(mid[q], weights[3 + j] * line[q])
                mid[3] = plus(mid[3], weights[3 + j] * line[4])
                mid[4] = plus(mid[4], slope[3 + j] * line[3])
                mid[5] = plus(mid[5], weights[3 + j] * line[3])
            for q in range(5):
                sums[q] = plus(sums[q], weights[6 + k] * mid[q])
            sums[5] = plus(sums[5], slope[6 + k] * mid[5])
        for q in range(6):
            part[q, plane] = sums[q]
        return carry

    lax.fori_loop(0, BX, read, 0)

    for name in ("zi", "uf", "up"):
        loads[name].wait()
    for copy in w_copies:
        copy.wait_recv()
    spread = dot(jnp.concatenate([wrec[d] for d in range(ngx)], axis=1), local["zi"][...])
    value, slant = spread[:, 0:128], spread[:, 128:256]
    far = [
        dot(local["uf"][0], value),
        dot(local["uf"][1], value),
        dot(local["uf"][2], slant),
    ]
    fine = dot(local["up"][...], spread[:, 256:640])
    for k in range(3):
        psi[k] = fine[:, 128 * k : 128 * (k + 1)].reshape(inner, WY, 128)
    for axis in range(3):
        moved[axis] = SMAX * bent[axis] + STEP * (
            part[axis] + far[axis].reshape(BX, BY, 128)
        )

    def finish(plane, carry):
        weights, slope = slopes(plane)
        sums = [part[3 + axis, plane] for axis in range(3)]
        for k in range(3):
            mid = [None] * 3
            for j in range(3):
                line = [None] * 2
                for i in range(3):
                    at = psi[k, plane + i, pl.ds(j, BY), :]
                    line[0] = plus(line[0], weights[i] * at)
                    line[1] = plus(line[1], slope[i] * at)
                mid[0] = plus(mid[0], weights[3 + j] * line[1])
                mid[1] = plus(mid[1], slope[3 + j] * line[0])
                mid[2] = plus(mid[2], weights[3 + j] * line[0])
            sums[0] = sums[0] + weights[6 + k] * mid[0]
            sums[1] = sums[1] + weights[6 + k] * mid[1]
            sums[2] = sums[2] + slope[6 + k] * mid[2]
        for axis in range(3):
            bend = bent[axis, plane]
            grad[axis, plane] = (cot[axis, plane] + sums[axis]) * (SMAX * (1.0 - bend * bend))
        return carry

    lax.fori_loop(0, BX, finish, 0)
    for copy in started:
        copy.wait_send()


def body(tables, sizes, latent, cotangent):
    ngx, ngy, ngz = sizes
    dma = pltpu.SemaphoreType.DMA
    f32 = jnp.float32

    def vmem(*shape):
        return pltpu.VMEM(shape, f32)

    arrays = [jnp.asarray(tables[name]) for name in NAMES]
    locals_ = [
        vmem(*(array.shape[1:] if name in AXIS_OF else array.shape))
        for name, array in zip(NAMES, arrays)
    ]
    scratch = [
        vmem(3, BX, BY, 128),
        vmem(9, 12, 32, 128),
        vmem(3, 12, 32, 128),
        vmem(9, 14, 40, 128),
        vmem(2, WX, WY, 128),
        vmem(2, WX, WY, 128),
        vmem(2, WY, 128),
        vmem(2, 2, WY, 128),
        vmem(2, 2, WY, 128),
        vmem(2, 2, 12, 8, 128),
        vmem(2, 2, 8, 128),
        vmem(2, 2, 5, WY, 128),
        vmem(2, 2, WY, 128),
        vmem(ngx, 64, 128),
        vmem(ngx, 64, 128),
        vmem(ngz, 48, 128),
        vmem(ngz, 48, 128),
        vmem(ngy, 48, 128),
        vmem(ngz, 48, 128),
        vmem(ngx, 64, 128),
        vmem(4, 3, BX + 2, WY, 128),
        vmem(3, BX + 2, WY, 128),
        vmem(6, BX, BY, 128),
        dma((len(NAMES),)),
        dma((ngx,)), dma((ngx,)),
        dma((ngz,)), dma((ngz,)),
        dma((ngz,)), dma((ngz,)),
        dma((ngx,)), dma((ngx,)),
        dma((ngy,)), dma((ngy,)),
        dma((12,)), dma((12,)),
    ]
    whole = pl.BlockSpec(memory_space=pltpu.VMEM)
    return pl.pallas_call(
        functools.partial(kernel, sizes),
        out_shape=[jax.ShapeDtypeStruct((3, BX, BY, BZ), f32)] * 2,
        in_specs=[whole, whole] + [pl.BlockSpec(memory_space=pl.ANY)] * len(NAMES),
        out_specs=[whole, whole],
        scratch_shapes=locals_ + scratch,
        compiler_params=pltpu.CompilerParams(
            collective_id=0, has_side_effects=True, vmem_limit_bytes=48 * 1024 * 1024
        ),
    )(latent, cotangent, *arrays)


def solution(mesh):
    sizes = (mesh.shape["gx"], mesh.shape["gy"], mesh.shape["gz"])
    tables = make_tables(*sizes)
    placed = P(None, "gy", "gz", "gx")
    return jax.shard_map(
        functools.partial(body, tables, sizes),
        mesh=mesh,
        in_specs=(placed, placed),
        out_specs=(placed, placed),
        check_vma=False,
    )
```

profile of v0, /device:TPU:33, one launch (start us, length us, event | category | flops | bytes accessed | tf_op | source)
XLA Modules:
  0.0 60.2 jit_solution(17188857362814140531)
XLA Ops:
  0.6 0.0 copy-start
  0.6 1.2 %copy-done = f32[3,240,384]{2,1,0:T(8,128)S(1)} copy-done((f32[3,240,384]{2,1,0:T(8,128)S(1)}, f32[3,240,384]{2,1,0:T(8,128)}, u32[]{:S(2)}) %copy-start) | copy-done | bytes 1105944
  1.9 0.0 copy-start.1
  1.9 1.2 %copy-done.1 = f32[8,256,128]{2,1,0:T(8,128)S(1)} copy-done((f32[8,256,128]{2,1,0:T(8,128)S(1)}, f32[8,256,128]{2,1,0:T(8,128)}, u32[]{:S(2)}) %copy-start.1) | copy-done | bytes 1048600
  3.1 0.0 copy-start.2
  3.1 1.1 %copy-done.2 = f32[256,768]{1,0:T(8,128)S(1)} copy-done((f32[256,768]{1,0:T(8,128)S(1)}, f32[256,768]{1,0:T(8,128)}, u32[]{:S(2)}) %copy-start.2) | copy-done | bytes 786456
  4.2 0.0 copy-start.3
  4.2 1.1 %copy-done.3 = f32[8,64,384]{2,1,0:T(8,128)S(1)} copy-done((f32[8,64,384]{2,1,0:T(8,128)S(1)}, f32[8,64,384]{2,1,0:T(8,128)}, u32[]{:S(2)}) %copy-start.3) | copy-done | bytes 786456
  5.4 0.0 copy-start.4
  5.4 1.0 %copy-done.4 = f32[8,48,256]{2,1,0:T(8,128)S(1)} copy-done((f32[8,48,256]{2,1,0:T(8,128)S(1)}, f32[8,48,256]{2,1,0:T(8,128)}, u32[]{:S(2)}) %copy-start.4) | copy-done | bytes 393240
  6.4 0.0 copy-start.5
  6.4 1.0 %copy-done.5 = f32[256,384]{1,0:T(8,128)S(1)} copy-done((f32[256,384]{1,0:T(8,128)S(1)}, f32[256,384]{1,0:T(8,128)}, u32[]{:S(2)}) %copy-start.5) | copy-done | bytes 393240
  7.4 0.0 copy-start.6
  7.4 0.9 %copy-done.6 = f32[3,8,16,128]{3,2,1,0:T(8,128)S(1)} copy-done((f32[3,8,16,128]{3,2,1,0:T(8,128)S(1)}, f32[3,8,16,128]{3,2,1,0:T(8,128)}, u32[]{:S(2)}) %copy-start.6) | copy-done | bytes 196632
  8.3 0.0 copy-start.7
  8.3 0.9 %copy-done.7 = f32[3,8,16,128]{3,2,1,0:T(8,128)S(1)} copy-done((f32[3,8,16,128]{3,2,1,0:T(8,128)S(1)}, f32[3,8,16,128]{3,2,1,0:T(8,128)}, u32[]{:S(2)}) %copy-start.7) | copy-done | bytes 196632
  9.2 0.0 copy-start.8
  9.2 0.9 %copy-done.8 = f32[3,128,64]{2,1,0:T(8,128)S(1)} copy-done((f32[3,128,64]{2,1,0:T(8,128)S(1)}, f32[3,128,64]{2,1,0:T(8,128)}, u32[]{:S(2)}) %copy-start.8) | copy-done | bytes 98328
  10.1 0.0 copy-start.9
  10.1 0.9 %copy-done.9 = f32[240,64]{1,0:T(8,128)S(1)} copy-done((f32[240,64]{1,0:T(8,128)S(1)}, f32[240,64]{1,0:T(8,128)}, u32[]{:S(2)}) %copy-start.9) | copy-done | bytes 61464
  11.0 0.0 copy-start.10
  11.0 0.9 %copy-done.10 = f32[64,384]{1,0:T(8,128)S(1)} copy-done((f32[64,384]{1,0:T(8,128)S(1)}, f32[64,384]{1,0:T(8,128)}, u32[]{:S(2)}) %copy-start.10) | copy-done | bytes 98328
  11.9 0.0 copy-start.11
  11.9 0.8 %copy-done.11 = f32[64,240]{1,0:T(8,128)S(1)} copy-done((f32[64,240]{1,0:T(8,128)S(1)}, f32[64,240]{1,0:T(8,128)}, u32[]{:S(2)}) %copy-start.11) | copy-done | bytes 61464
  12.8 0.0 copy-start.12
  12.8 0.7 %copy-done.12 = f32[4,8,128]{2,1,0:T(8,128)S(1)} copy-done((f32[4,8,128]{2,1,0:T(8,128)S(1)}, f32[4,8,128]{2,1,0:T(8,128)}, u32[]{:S(2)}) %copy-start.12) | copy-done | bytes 16408
  13.5 45.3 %shard_map.167 = (f32[3,8,16,128]{3,2,1,0:T(8,128)S(1)}, f32[3,8,16,128]{3,2,1,0:T(8,128)S(1)}) custom-call(f32[3,8,16,128]{3,2,1,0:T(8,128)S(1)} %copy-done.6, f32[3,8,16,128]{3,2,1,0:T(8,128)S(1)} %copy-done.7, f32[64,240]{1,0:T(8,128)S(1)} %copy-done.11, f32[64,384]{1,0:T(8,128)S(1)} %copy-done.10, f32[4,512,512]{2,1,0:T(8,128)} %constant.30.clone.refs_2_, ...), custom_call_target="tpu_custom_call" | custom-call | tf_op jit(solution)/shard_map/pallas_call | solution.py:589
  58.8 0.7 %copy.20 = f32[3,8,16,128]{3,2,1,0:T(8,128)} copy(f32[3,8,16,128]{3,2,1,0:T(8,128)S(1)} %get-tuple-element.4) | data formatting | bytes 393216
  59.5 0.7 %copy.21 = f32[3,8,16,128]{3,2,1,0:T(8,128)} copy(f32[3,8,16,128]{3,2,1,0:T(8,128)S(1)} %get-tuple-element.5) | data formatting | bytes 393216
Async XLA Ops:
  0.6 1.2 %copy-start = (f32[3,240,384]{2,1,0:T(8,128)S(1)}, f32[3,240,384]{2,1,0:T(8,128)}, u32[]{:S(2)}) copy-start(f32[3,240,384]{2,1,0:T(8,128)} %constant.41.clone.refs_13_) | copy-start | bytes 3317764
  1.9 1.2 %copy-start.1 = (f32[8,256,128]{2,1,0:T(8,128)S(1)}, f32[8,256,128]{2,1,0:T(8,128)}, u32[]{:S(2)}) copy-start(f32[8,256,128]{2,1,0:T(8,128)} %constant.34.clone.refs_6_) | copy-start | bytes 3145732
  3.1 1.1 %copy-start.2 = (f32[256,768]{1,0:T(8,128)S(1)}, f32[256,768]{1,0:T(8,128)}, u32[]{:S(2)}) copy-start(f32[256,768]{1,0:T(8,128)} %constant.40.clone.refs_12_) | copy-start | bytes 2359300
  4.2 1.1 %copy-start.3 = (f32[8,64,384]{2,1,0:T(8,128)S(1)}, f32[8,64,384]{2,1,0:T(8,128)}, u32[]{:S(2)}) copy-start(f32[8,64,384]{2,1,0:T(8,128)} %constant.36.clone.refs_8_) | copy-start | bytes 2359300
  5.4 1.0 %copy-start.4 = (f32[8,48,256]{2,1,0:T(8,128)S(1)}, f32[8,48,256]{2,1,0:T(8,128)}, u32[]{:S(2)}) copy-start(f32[8,48,256]{2,1,0:T(8,128)} %constant.33.clone.refs_5_) | copy-start | bytes 1179652
  6.4 1.0 %copy-start.5 = (f32[256,384]{1,0:T(8,128)S(1)}, f32[256,384]{1,0:T(8,128)}, u32[]{:S(2)}) copy-start(f32[256,384]{1,0:T(8,128)} %constant.32.clone.refs_4_) | copy-start | bytes 1179652
  7.4 0.9 %copy-start.6 = (f32[3,8,16,128]{3,2,1,0:T(8,128)S(1)}, f32[3,8,16,128]{3,2,1,0:T(8,128)}, u32[]{:S(2)}) copy-start(f32[3,8,16,128]{3,2,1,0:T(8,128)} %lat.1) | copy-start | bytes 589828
  8.3 0.9 %copy-start.7 = (f32[3,8,16,128]{3,2,1,0:T(8,128)S(1)}, f32[3,8,16,128]{3,2,1,0:T(8,128)}, u32[]{:S(2)}) copy-start(f32[3,8,16,128]{3,2,1,0:T(8,128)} %cot.1) | copy-start | bytes 589828
  9.2 0.9 %copy-start.8 = (f32[3,128,64]{2,1,0:T(8,128)S(1)}, f32[3,128,64]{2,1,0:T(8,128)}, u32[]{:S(2)}) copy-start(f32[3,128,64]{2,1,0:T(8,128)} %constant.38.clone.refs_10_) | copy-start | bytes 294916
  10.1 0.9 %copy-start.9 = (f32[240,64]{1,0:T(8,128)S(1)}, f32[240,64]{1,0:T(8,128)}, u32[]{:S(2)}) copy-start(f32[240,64]{1,0:T(8,128)} %constant.39.clone.refs_11_) | copy-start | bytes 184324
  11.0 0.9 %copy-start.10 = (f32[64,384]{1,0:T(8,128)S(1)}, f32[64,384]{1,0:T(8,128)}, u32[]{:S(2)}) copy-start(f32[64,384]{1,0:T(8,128)} %constant.29.clone.refs_1_) | copy-start | bytes 294916
  11.9 0.8 %copy-start.11 = (f32[64,240]{1,0:T(8,128)S(1)}, f32[64,240]{1,0:T(8,128)}, u32[]{:S(2)}) copy-start(f32[64,240]{1,0:T(8,128)} %constant.28.clone.refs_0_) | copy-start | bytes 184324
  12.8 0.7 %copy-start.12 = (f32[4,8,128]{2,1,0:T(8,128)S(1)}, f32[4,8,128]{2,1,0:T(8,128)}, u32[]{:S(2)}) copy-start(f32[4,8,128]{2,1,0:T(8,128)} %constant.35.clone.refs_7_) | copy-start | bytes 49156
where the time goes:
time: 60.7 us; the launch traced here: 60.2 us
  Pallas kernels  45.3 us (75%)
  local copies, waits for them, and re-layouts  14.2 us (23%)
  between operations  0.66 us (1%)
    pallas_call x1, Pallas kernels, body(): pl.pallas_call(functools.partial(kernel, sizes), out_shape=[jax.ShapeDtyp...  45.3 us
    unnamed x28, local copies, waits for them, and re-layouts  14.2 us

commit v1 on v0

--- a/solution.py
+++ b/solution.py
@@ -3,6 +3,7 @@
 
 import jax
 import jax.numpy as jnp
+import ml_dtypes
 import numpy as np
 from jax import lax
 from jax.experimental import pallas as pl
@@ -139,16 +140,48 @@
             half * np.kron(kx(0), ky(0)),
         ]
     )
-    return {name: np.ascontiguousarray(value, dtype=np.float32) for name, value in f.items()}
-
-
-def dot(left, right):
-    return jnp.dot(
-        left, right, precision=lax.Precision.HIGHEST, preferred_element_type=jnp.float32
-    )
-
-
-NAMES = ("cd", "cp", "zt", "yt", "xf", "xi", "ka", "kb", "yi", "zi", "uf", "up", "sz", "an")
+    f["cq"], f["c0"] = f["cp"][:, 0:256], f.pop("cp")[:, 256:384]
+    tables = {}
+    for name, value in f.items():
+        if name not in AXIS_OF:
+            value = value[None]
+        value = value.astype(np.float32)
+        if name in LEFT or name in RIGHT:
+            high = value.astype(ml_dtypes.bfloat16)
+            low = (value - high.astype(np.float32)).astype(ml_dtypes.bfloat16)
+            value = np.concatenate([high, high, low], axis=-1 if name in LEFT else -2)
+        least = -(-TABLE_BYTES // value[0].nbytes)
+        filler = np.zeros((max(0, least - len(value)),) + value.shape[1:], value.dtype)
+        tables[name] = np.ascontiguousarray(np.concatenate([value, filler]))
+    return tables
+
+
+TABLE_BYTES = 2**21
+NAMES = (
+    "cd", "cq", "c0", "zt", "yt", "xf", "xi", "ka", "kb", "yi", "sz", "an", "zi", "uf", "up",
+)
+LEFT = ("cd", "cq", "c0", "yt", "xf", "xi", "yi", "uf", "up", "an")
+RIGHT = ("zt", "zi", "sz")
+
+
+def halves(value):
+    high = value.astype(jnp.bfloat16)
+    low = (value - high.astype(jnp.float32)).astype(jnp.bfloat16)
+    return high, low
+
+
+def dot(table, value):
+    high, low = halves(value)
+    stacked = jnp.concatenate([high, low, high], axis=0)
+    return jnp.dot(table, stacked, preferred_element_type=jnp.float32)
+
+
+def rdot(value, table):
+    high, low = halves(value)
+    stacked = jnp.concatenate([high, low, high], axis=1)
+    return jnp.dot(stacked, table, preferred_element_type=jnp.float32)
+
+
 AXIS_OF = {"zt": "gx", "yt": "gz", "xi": "gy", "ka": "gz", "kb": "gx", "yi": "gz", "zi": "gx"}
 
 
@@ -169,9 +202,7 @@
 
     loads = {}
     for number, name in enumerate(NAMES):
-        source = tables[name]
-        if name in AXIS_OF:
-            source = source.at[place[AXIS_OF[name]]]
+        source = tables[name].at[place[AXIS_OF[name]] if name in AXIS_OF else 0]
         loads[name] = pltpu.make_async_copy(source, local[name], table_sem.at[number])
         loads[name].start()
 
@@ -244,17 +275,18 @@
     lax.fori_loop(0, BX + 2, paint, 0)
 
     loads["cd"].wait()
-    loads["cp"].wait()
+    loads["cq"].wait()
+    loads["c0"].wait()
     inner = BX + 2
     density = jnp.concatenate(
         [f0[0, 3:13].reshape(inner * WY, 128), t1[0, 3:13].reshape(inner * WY, 128)], axis=1
     )
     rho = dot(local["cd"][...], density)
     pushed = [(STEP * cot[axis]).reshape(BX * BY, 128) for axis in range(3)]
-    cross_source = dot(local["cp"][:, 0:256], jnp.concatenate(pushed[:2], axis=0))
-    along_source = dot(local["cp"][:, 256:384], pushed[2])
+    cross_source = dot(local["cq"][...], jnp.concatenate(pushed[:2], axis=0))
+    along_source = dot(local["c0"][...], pushed[2])
     loads["zt"].wait()
-    modes = dot(jnp.concatenate([rho, cross_source, along_source], axis=1), local["zt"][...])
+    modes = rdot(jnp.concatenate([rho, cross_source, along_source], axis=1), local["zt"][...])
     for j in range(ngx):
         zbuf[j] = modes[:, 128 * j : 128 * (j + 1)]
     pl.semaphore_wait(barrier, len(partners))
@@ -437,11 +469,11 @@
         for k in range(3):
             target[slot, k] = value[:, 128 * k : 128 * (k + 1)].reshape(inner, WY, 128)
 
-    smoothed = dot(window[0], local["sz"][:, 0:384])
+    smoothed = rdot(window[0], local["sz"][:, 0:384])
     keep(near, 0, dot(local["an"][0], smoothed))
     keep(near, 1, dot(local["an"][1], smoothed))
-    keep(near, 2, dot(local["an"][2], dot(window[0], local["sz"][:, 384:768])))
-    keep(near, 3, -2.0 * dot(local["an"][2], dot(window[1], local["sz"][:, 0:384])))
+    keep(near, 2, dot(local["an"][2], rdot(window[0], local["sz"][:, 384:768])))
+    keep(near, 3, -2.0 * dot(local["an"][2], rdot(window[1], local["sz"][:, 0:384])))
 
     loads["yi"].wait()
     for copy in u_copies:
@@ -498,7 +530,7 @@
         loads[name].wait()
     for copy in w_copies:
         copy.wait_recv()
-    spread = dot(jnp.concatenate([wrec[d] for d in range(ngx)], axis=1), local["zi"][...])
+    spread = rdot(jnp.concatenate([wrec[d] for d in range(ngx)], axis=1), local["zi"][...])
     value, slant = spread[:, 0:128], spread[:, 128:256]
     far = [
         dot(local["uf"][0], value),
@@ -550,8 +582,8 @@
 
     arrays = [jnp.asarray(tables[name]) for name in NAMES]
     locals_ = [
-        vmem(*(array.shape[1:] if name in AXIS_OF else array.shape))
-        for name, array in zip(NAMES, arrays)
+        pltpu.VMEM(array.shape[1:], array.dtype)
+        for array in arrays
     ]
     scratch = [
         vmem(3, BX, BY, 128),
@@ -593,7 +625,7 @@
         out_specs=[whole, whole],
         scratch_shapes=locals_ + scratch,
         compiler_params=pltpu.CompilerParams(
-            collective_id=0, has_side_effects=True, vmem_limit_bytes=48 * 1024 * 1024
+            collective_id=0, has_side_effects=True, vmem_limit_bytes=52 * 1024 * 1024
         ),
     )(latent, cotangent, *arrays)
 

time: 60.7 us -> 44.1 us (0.73)
  the two profiles are of different devices: /device:TPU:33 before, /device:TPU:1 now
where the time goes in v1:
time: 44.1 us; the launch traced here: 43.5 us
  Pallas kernels  39.6 us (90%)
  local copies, waits for them, and re-layouts  3.2 us (7%)
  between operations  0.65 us (1%)
    pallas_call x1, Pallas kernels, body(): pl.pallas_call(functools.partial(kernel, sizes), out_shape=[jax.ShapeDtyp...  39.6 us
    unnamed x6, local copies, waits for them, and re-layouts  3.2 us

profile of v1, /device:TPU:1, one launch (start us, length us, event | category | flops | bytes accessed | tf_op | source)
XLA Modules:
  0.0 43.5 jit_solution(3897777835721236177)
XLA Ops:
  0.6 0.0 copy-start
  0.6 0.9 %copy-done = f32[3,8,16,128]{3,2,1,0:T(8,128)S(1)} copy-done((f32[3,8,16,128]{3,2,1,0:T(8,128)S(1)}, f32[3,8,16,128]{3,2,1,0:T(8,128)}, u32[]{:S(2)}) %copy-start) | copy-done | bytes 196632
  1.6 0.0 copy-start.1
  1.6 0.9 %copy-done.1 = f32[3,8,16,128]{3,2,1,0:T(8,128)S(1)} copy-done((f32[3,8,16,128]{3,2,1,0:T(8,128)S(1)}, f32[3,8,16,128]{3,2,1,0:T(8,128)}, u32[]{:S(2)}) %copy-start.1) | copy-done | bytes 196632
  2.5 39.6 %shard_map.176 = (f32[3,8,16,128]{3,2,1,0:T(8,128)S(1)}, f32[3,8,16,128]{3,2,1,0:T(8,128)S(1)}) custom-call(f32[3,8,16,128]{3,2,1,0:T(8,128)S(1)} %copy-done, f32[3,8,16,128]{3,2,1,0:T(8,128)S(1)} %copy-done.1, bf16[23,64,720]{2,1,0:T(8,128)(2,1)} %constant.30.clone.refs_0_, bf16[22,64,768]{2,1,0:T(8,128)(2,1)} %constant.31.clone.refs_1_, ...), custom_call_target="tpu_custom_call" | custom-call | tf_op jit(solution)/shard_map/pallas_call | solution.py:621
  42.1 0.7 %copy.21 = f32[3,8,16,128]{3,2,1,0:T(8,128)} copy(f32[3,8,16,128]{3,2,1,0:T(8,128)S(1)} %get-tuple-element.4) | data formatting | bytes 393216
  42.8 0.7 %copy.22 = f32[3,8,16,128]{3,2,1,0:T(8,128)} copy(f32[3,8,16,128]{3,2,1,0:T(8,128)S(1)} %get-tuple-element.5) | data formatting | bytes 393216
Async XLA Ops:
  0.6 0.9 %copy-start = (f32[3,8,16,128]{3,2,1,0:T(8,128)S(1)}, f32[3,8,16,128]{3,2,1,0:T(8,128)}, u32[]{:S(2)}) copy-start(f32[3,8,16,128]{3,2,1,0:T(8,128)} %lat.1) | copy-start | bytes 589828
  1.6 0.9 %copy-start.1 = (f32[3,8,16,128]{3,2,1,0:T(8,128)S(1)}, f32[3,8,16,128]{3,2,1,0:T(8,128)}, u32[]{:S(2)}) copy-start(f32[3,8,16,128]{3,2,1,0:T(8,128)} %cot.1) | copy-start | bytes 589828

commit v2 on v1

--- a/solution.py
+++ b/solution.py
@@ -101,14 +101,15 @@
             for y in range(10):
                 yi[b, x * 10 + y, :, x, :] = qy[(CY * b + y - 1) % my].reshape(ngz, CY)
     f["yi"] = yi.reshape(ngz, 64, ngz * 48)
-    zi = np.zeros((ngx, ngx, 2, CZ, 640))
+    beside = lambda node: down(node) + np.where(node % 2 == 0, -1, 1)
+    zi = np.zeros((ngx, ngx, 2, CZ, 512))
     for c in range(ngx):
         at = lambda cell: qz[(CZ * c + cell) % mz].T.reshape(ngx, CZ, 128)
         zi[c, :, 0, :, 0:128] = at(down(oz))
         zi[c, :, 0, :, 128:256] = 0.5 * (at(down(oz) + 1) - at(down(oz) - 1))
-        for k in range(3):
-            zi[c, :, 1, :, 256 + 128 * k : 384 + 128 * k] = at(down(oz + k - 1))
-    f["zi"] = zi.reshape(ngx, ngx * 128, 640)
+        zi[c, :, 1, :, 256:384] = at(down(oz))
+        zi[c, :, 1, :, 384:512] = at(beside(oz))
+    f["zi"] = zi.reshape(ngx, ngx * 128, 512)
     pad4 = lambda matrix: np.concatenate([matrix, np.zeros((matrix.shape[0], 4))], axis=1)
     f["uf"] = np.stack(
         [
@@ -119,7 +120,12 @@
     )
     ry = np.arange(-1, WY - 1)
     row = ((ry <= BY) * 1.0)[:, None]
-    f["up"] = pad4(np.kron(same(down(fx), cxe), same(down(ry), cye) * row))
+    cells = (down, beside)
+    f["up"] = pad4(
+        np.concatenate(
+            [np.kron(same(p(ox), cxe), same(q(oy), cye)) for p in cells for q in cells]
+        )
+    )
     zw = np.concatenate([oz, oz + 128])
     zw[252:256] = np.arange(-4, 0)
     valid = np.concatenate([np.ones(128), np.ones(4), np.zeros(120), np.ones(4)])[:, None]
@@ -185,34 +191,39 @@
 AXIS_OF = {"zt": "gx", "yt": "gz", "xi": "gy", "ka": "gz", "kb": "gx", "yi": "gz", "zi": "gx"}
 
 
-def kernel(sizes, lat, cot, *refs):
+def kernel(sizes, lat_hbm, cot_hbm, *refs):
     ngx, ngy, ngz = sizes
     tables = dict(zip(NAMES, refs[: len(NAMES)]))
     moved, grad = refs[len(NAMES) : len(NAMES) + 2]
     rest = refs[len(NAMES) + 2 :]
     local = dict(zip(NAMES, rest[: len(NAMES)]))
     (
-        bent, wt, vals, bk, f0, t1, hp, tsend, trecv, yrecv, yhrecv, xrecv, xhrecv,
+        lat, cot, cell, bent, wt, vals, bk, f0, t1, hp, tsend, trecv, yrecv, yhrecv, xrecv, xhrecv,
         zbuf, zrecv, ybuf, yrec, xrec, urec, wrec, near, psi, part,
-        table_sem, s_z, r_z, s_y, r_y, s_u, r_u, s_w, r_w, s_x, r_x, s_h, r_h,
+        table_sem, arg_sem, s_z, r_z, s_y, r_y, s_u, r_u, s_w, r_w, s_x, r_x, s_h, r_h,
     ) = rest[len(NAMES) :]
     c, a, b = lax.axis_index("gx"), lax.axis_index("gy"), lax.axis_index("gz")
     place = {"gx": c, "gy": a, "gz": b}
     size = {"gx": ngx, "gy": ngy, "gz": ngz}
 
+    def other(axis, step):
+        return {axis: lax.rem(place[axis] + step, size[axis])}
+
+    arguments = [
+        pltpu.make_async_copy(lat_hbm, lat, arg_sem.at[0]),
+        pltpu.make_async_copy(cot_hbm, cot, arg_sem.at[1]),
+    ]
+    for copy in arguments:
+        copy.start()
+    barrier = pltpu.get_barrier_semaphore()
+    partners = [(axis, step) for axis in size for step in range(1, size[axis])]
+    for axis, step in partners:
+        pl.semaphore_signal(barrier, inc=1, device_id=other(axis, step), device_id_type=MESH)
     loads = {}
     for number, name in enumerate(NAMES):
         source = tables[name].at[place[AXIS_OF[name]] if name in AXIS_OF else 0]
         loads[name] = pltpu.make_async_copy(source, local[name], table_sem.at[number])
         loads[name].start()
-
-    def other(axis, step):
-        return {axis: lax.rem(place[axis] + step, size[axis])}
-
-    barrier = pltpu.get_barrier_semaphore()
-    partners = [(axis, step) for axis in size for step in range(1, size[axis])]
-    for axis, step in partners:
-        pl.semaphore_signal(barrier, inc=1, device_id=other(axis, step), device_id_type=MESH)
 
     started = []
 
@@ -233,11 +244,7 @@
     upper = lax.rem(lane, 8) >= 4
 
     wt[...] = jnp.zeros_like(wt)
-    f0[...] = jnp.zeros_like(f0)
-    t1[...] = jnp.zeros_like(t1)
-    hp[...] = jnp.zeros_like(hp)
-    vals[...] = jnp.zeros_like(vals)
-    bk[...] = jnp.zeros_like(bk)
+    arguments[0].wait()
     for axis in range(3):
         bend = jnp.tanh(lat[axis])
         bent[axis] = bend
@@ -245,7 +252,6 @@
         wt[3 * axis, 2:10, 8:24] = 0.5 * (0.5 - shift) ** 2
         wt[3 * axis + 1, 2:10, 8:24] = 0.75 - shift * shift
         wt[3 * axis + 2, 2:10, 8:24] = 0.5 * (0.5 + shift) ** 2
-        vals[axis, 2:10, 8:24] = STEP * cot[axis]
 
     def gathered(plane, charges):
         totals = [[None] * 3 for _ in range(charges or 1)]
@@ -282,6 +288,7 @@
         [f0[0, 3:13].reshape(inner * WY, 128), t1[0, 3:13].reshape(inner * WY, 128)], axis=1
     )
     rho = dot(local["cd"][...], density)
+    arguments[1].wait()
     pushed = [(STEP * cot[axis]).reshape(BX * BY, 128) for axis in range(3)]
     cross_source = dot(local["cq"][...], jnp.concatenate(pushed[:2], axis=0))
     along_source = dot(local["c0"][...], pushed[2])
@@ -295,6 +302,17 @@
         for d in range(1, ngx)
     ]
     started += z_copies
+
+    f0[0, 0:3] = jnp.zeros((3, WY, 128), jnp.float32)
+    f0[0, 13:16] = jnp.zeros((3, WY, 128), jnp.float32)
+    t1[0, 0:3] = jnp.zeros((3, WY, 128), jnp.float32)
+    t1[0, 13:16] = jnp.zeros((3, WY, 128), jnp.float32)
+    f0[1] = jnp.zeros((WX, WY, 128), jnp.float32)
+    t1[1] = jnp.zeros((WX, WY, 128), jnp.float32)
+    vals[...] = jnp.zeros_like(vals)
+    bk[...] = jnp.zeros_like(bk)
+    for axis in range(3):
+        vals[axis, 2:10, 8:24] = STEP * cot[axis]
 
     def paint_back(plane, carry):
         totals = gathered(plane, 3)
@@ -436,6 +454,15 @@
     ]
     started += u_copies
 
+    loads["yi"].wait()
+    for copy in u_copies:
+        copy.wait_recv()
+    wrec[c] = dot(local["yi"][...], urec[...].reshape(ngz * 48, 128))
+    w_copies = [
+        send(wrec.at[c], wrec.at[c], s_w.at[d], r_w.at[d], "gx", d) for d in range(1, ngx)
+    ]
+    started += w_copies
+
     for copy in side_copies:
         copy.wait()
     f0[0, 0:5] = f0[0, 0:5] + xrecv[0, 0]
@@ -475,15 +502,6 @@
     keep(near, 2, dot(local["an"][2], rdot(window[0], local["sz"][:, 384:768])))
     keep(near, 3, -2.0 * dot(local["an"][2], rdot(window[1], local["sz"][:, 0:384])))
 
-    loads["yi"].wait()
-    for copy in u_copies:
-        copy.wait_recv()
-    wrec[c] = dot(local["yi"][...], urec[...].reshape(ngz * 48, 128))
-    w_copies = [
-        send(wrec.at[c], wrec.at[c], s_w.at[d], r_w.at[d], "gx", d) for d in range(1, ngx)
-    ]
-    started += w_copies
-
     def slopes(plane):
         rows = pl.ds(8, BY)
         weights = [wt[n, plane + 2, rows, :] for n in range(9)]
@@ -495,6 +513,9 @@
 
     def plus(total, term):
         return term if total is None else total + term
+
+    even_row = lax.rem(lax.broadcasted_iota(jnp.int32, (BY, 128), 0), 2) == 0
+    even_lane = lax.rem(lax.broadcasted_iota(jnp.int32, (BY, 128), 1), 2) == 0
 
     def read(plane, carry):
         weights, slope = slopes(plane)
@@ -522,6 +543,13 @@
             sums[5] = plus(sums[5], slope[6 + k] * mid[5])
         for q in range(6):
             part[q, plane] = sums[q]
+        even = (lax.rem(plane, 2) == 0, even_row, even_lane)
+        for axis in range(3):
+            for n, (low, mid, high) in enumerate(
+                (weights[3 * axis : 3 * axis + 3], slope[3 * axis : 3 * axis + 3])
+            ):
+                cell[4 * axis + 2 * n, plane] = mid + jnp.where(even[axis], high, low)
+                cell[4 * axis + 2 * n + 1, plane] = jnp.where(even[axis], low, high)
         return carry
 
     lax.fori_loop(0, BX, read, 0)
@@ -537,31 +565,29 @@
         dot(local["uf"][1], value),
         dot(local["uf"][2], slant),
     ]
-    fine = dot(local["up"][...], spread[:, 256:640])
-    for k in range(3):
-        psi[k] = fine[:, 128 * k : 128 * (k + 1)].reshape(inner, WY, 128)
+    fine = dot(local["up"][...], spread[:, 256:512])
+    for k in range(2):
+        psi[k] = fine[:, 128 * k : 128 * (k + 1)].reshape(4, BX, BY, 128)
     for axis in range(3):
         moved[axis] = SMAX * bent[axis] + STEP * (
             part[axis] + far[axis].reshape(BX, BY, 128)
         )
 
     def finish(plane, carry):
-        weights, slope = slopes(plane)
         sums = [part[3 + axis, plane] for axis in range(3)]
-        for k in range(3):
+        group = [cell[n, plane] for n in range(12)]
+        for k in range(2):
             mid = [None] * 3
-            for j in range(3):
-                line = [None] * 2
-                for i in range(3):
-                    at = psi[k, plane + i, pl.ds(j, BY), :]
-                    line[0] = plus(line[0], weights[i] * at)
-                    line[1] = plus(line[1], slope[i] * at)
-                mid[0] = plus(mid[0], weights[3 + j] * line[1])
-                mid[1] = plus(mid[1], slope[3 + j] * line[0])
-                mid[2] = plus(mid[2], weights[3 + j] * line[0])
-            sums[0] = sums[0] + weights[6 + k] * mid[0]
-            sums[1] = sums[1] + weights[6 + k] * mid[1]
-            sums[2] = sums[2] + slope[6 + k] * mid[2]
+            for j in range(2):
+                here, there = psi[k, j, plane], psi[k, 2 + j, plane]
+                line = group[0] * here + group[1] * there
+                tilt = group[2] * here + group[3] * there
+                mid[0] = plus(mid[0], group[4 + j] * tilt)
+                mid[1] = plus(mid[1], group[6 + j] * line)
+                mid[2] = plus(mid[2], group[4 + j] * line)
+            sums[0] = sums[0] + group[8 + k] * mid[0]
+            sums[1] = sums[1] + group[8 + k] * mid[1]
+            sums[2] = sums[2] + group[10 + k] * mid[2]
         for axis in range(3):
             bend = bent[axis, plane]
             grad[axis, plane] = (cot[axis, plane] + sums[axis]) * (SMAX * (1.0 - bend * bend))
@@ -586,6 +612,9 @@
         for array in arrays
     ]
     scratch = [
+        vmem(3, BX, BY, 128),
+        vmem(3, BX, BY, 128),
+        vmem(12, BX, BY, 128),
         vmem(3, BX, BY, 128),
         vmem(9, 12, 32, 128),
         vmem(3, 12, 32, 128),
@@ -607,9 +636,10 @@
         vmem(ngz, 48, 128),
         vmem(ngx, 64, 128),
         vmem(4, 3, BX + 2, WY, 128),
-        vmem(3, BX + 2, WY, 128),
+        vmem(2, 4, BX, BY, 128),
         vmem(6, BX, BY, 128),
         dma((len(NAMES),)),
+        dma((2,)),
         dma((ngx,)), dma((ngx,)),
         dma((ngz,)), dma((ngz,)),
         dma((ngz,)), dma((ngz,)),
@@ -621,11 +651,11 @@
     return pl.pallas_call(
         functools.partial(kernel, sizes),
         out_shape=[jax.ShapeDtypeStruct((3, BX, BY, BZ), f32)] * 2,
-        in_specs=[whole, whole] + [pl.BlockSpec(memory_space=pl.ANY)] * len(NAMES),
+        in_specs=[pl.BlockSpec(memory_space=pl.ANY)] * (2 + len(NAMES)),
         out_specs=[whole, whole],
         scratch_shapes=locals_ + scratch,
         compiler_params=pltpu.CompilerParams(
-            collective_id=0, has_side_effects=True, vmem_limit_bytes=52 * 1024 * 1024
+            collective_id=0, has_side_effects=True, vmem_limit_bytes=54784 * 1024
         ),
     )(latent, cotangent, *arrays)
 

time: 44.1 us -> 42.8 us (0.971); the launches traced: 43.5 us -> 42.7 us
  local copies, waits for them, and re-layouts: 3.2 us -> 1.36 us
  Pallas kernels: 39.6 us -> 40.7 us
    unnamed x6 -> x2, local copies, waits for them, and re-layouts: 3.2 us -> 1.36 us
    pallas_call x1, Pallas kernels: 39.6 us -> 40.7 us  [body(): pl.pallas_call(functools.partial(kernel, sizes), out_shape=[jax.ShapeDtyp...]
where the time goes in v2:
time: 42.8 us; the launch traced here: 42.7 us
  Pallas kernels  40.7 us (95%)
  local copies, waits for them, and re-layouts  1.36 us (3%)
  between operations  0.64 us (1%)
    pallas_call x1, Pallas kernels, body(): pl.pallas_call(functools.partial(kernel, sizes), out_shape=[jax.ShapeDtyp...  40.7 us
    unnamed x2, local copies, waits for them, and re-layouts  1.36 us

profile of v2, /device:TPU:1, one launch (start us, length us, event | category | flops | bytes accessed | tf_op | source)
XLA Modules:
  0.0 42.7 jit_solution(13044434706476040315)
XLA Ops:
  0.6 40.7 %shard_map.176 = (f32[3,8,16,128]{3,2,1,0:T(8,128)S(1)}, f32[3,8,16,128]{3,2,1,0:T(8,128)S(1)}) custom-call(f32[3,8,16,128]{3,2,1,0:T(8,128)} %lat_hbm.1, f32[3,8,16,128]{3,2,1,0:T(8,128)} %cot_hbm.1, bf16[23,64,720]{2,1,0:T(8,128)(2,1)} %constant.30.clone.refs_0_, bf16[22,64,768]{2,1,0:T(8,128)(2,1)} %constant.31.clone.refs_1_, ...), custom_call_target="tpu_custom_call" | custom-call | tf_op jit(solution)/shard_map/pallas_call | solution.py:651
  41.3 0.7 %copy.21 = f32[3,8,16,128]{3,2,1,0:T(8,128)} copy(f32[3,8,16,128]{3,2,1,0:T(8,128)S(1)} %get-tuple-element.4) | data formatting | bytes 393216
  42.0 0.7 %copy.22 = f32[3,8,16,128]{3,2,1,0:T(8,128)} copy(f32[3,8,16,128]{3,2,1,0:T(8,128)S(1)} %get-tuple-element.5) | data formatting | bytes 393216

commit v3 on v2

--- a/solution.py
+++ b/solution.py
@@ -130,9 +130,11 @@
     zw[252:256] = np.arange(-4, 0)
     valid = np.concatenate([np.ones(128), np.ones(4), np.zeros(120), np.ones(4)])[:, None]
     tap = lambda target, extra: five(target[None, :] + extra - zw[:, None]) * valid
+    own, past = oz, np.where(oz == 0, BZ, -1)
+    ends = np.logical_or(oz == 0, oz == BZ - 1)[None, :]
     f["sz"] = np.concatenate(
-        [tap(oz + k, 0) for k in (-1, 0, 1)]
-        + [tap(oz + k, 1) - tap(oz + k, -1) for k in (-1, 0, 1)],
+        [tap(own, 0), tap(past, 0) * ends]
+        + [tap(own, 1) - tap(own, -1), (tap(past, 1) - tap(past, -1)) * ends],
         axis=1,
     )
     wx, wy = np.arange(-4, WX - 4), np.arange(-4, WY - 4)
@@ -427,6 +429,17 @@
     f0[:, 2:14, 16:24] = f0[:, 2:14, 16:24] + yrecv[1]
     hp[:, 0:8] = hp[:, 0:8] + yhrecv[0]
     hp[:, 16:24] = hp[:, 16:24] + yhrecv[1]
+    loads["ka"].wait()
+    loads["kb"].wait()
+    squares = local["ka"][...] + local["kb"][0:1, :]
+    zero = squares == 0.0
+    gain = jnp.where(
+        zero, 0.0, COUPLE * jnp.exp(-SPREAD * squares) / jnp.where(zero, 1.0, squares)
+    )
+    loads["xf"].wait()
+    loads["xi"].wait()
+    for copy in x_copies:
+        copy.wait_recv()
     side_copies = [
         send(f0.at[0, 8:13], xrecv.at[0, 0], s_h.at[6], r_h.at[6], "gy", 1),
         send(f0.at[1, 9:14], xrecv.at[0, 1], s_h.at[7], r_h.at[7], "gy", 1),
@@ -435,18 +448,6 @@
         send(hp, xhrecv.at[0], s_h.at[10], r_h.at[10], "gy", 1),
         send(hp, xhrecv.at[1], s_h.at[11], r_h.at[11], "gy", ngy - 1),
     ]
-
-    loads["ka"].wait()
-    loads["kb"].wait()
-    squares = local["ka"][...] + local["kb"][0:1, :]
-    zero = squares == 0.0
-    gain = jnp.where(
-        zero, 0.0, COUPLE * jnp.exp(-SPREAD * squares) / jnp.where(zero, 1.0, squares)
-    )
-    loads["xf"].wait()
-    loads["xi"].wait()
-    for copy in x_copies:
-        copy.wait_recv()
     spectrum = dot(local["xf"][...], xrec[...].reshape(ngy * 48, 128))
     urec[b] = dot(local["xi"][...], gain * spectrum)
     u_copies = [
@@ -492,15 +493,20 @@
     loads["sz"].wait()
     loads["an"].wait()
 
+    column = lax.broadcasted_iota(jnp.int32, (inner * WY, 128), 1)
+
     def keep(target, slot, value):
-        for k in range(3):
-            target[slot, k] = value[:, 128 * k : 128 * (k + 1)].reshape(inner, WY, 128)
-
-    smoothed = rdot(window[0], local["sz"][:, 0:384])
+        own, past = value[:, 0:128], value[:, 128:256]
+        before = jnp.where(column == 0, pltpu.roll(past, 1, 1), pltpu.roll(own, 1, 1))
+        after = jnp.where(column == 127, pltpu.roll(past, 127, 1), pltpu.roll(own, 127, 1))
+        for k, shifted in enumerate((before, own, after)):
+            target[slot, k] = shifted.reshape(inner, WY, 128)
+
+    smoothed = rdot(window[0], local["sz"][:, 0:256])
     keep(near, 0, dot(local["an"][0], smoothed))
     keep(near, 1, dot(local["an"][1], smoothed))
-    keep(near, 2, dot(local["an"][2], rdot(window[0], local["sz"][:, 384:768])))
-    keep(near, 3, -2.0 * dot(local["an"][2], rdot(window[1], local["sz"][:, 0:384])))
+    keep(near, 2, dot(local["an"][2], rdot(window[0], local["sz"][:, 256:512])))
+    keep(near, 3, -2.0 * dot(local["an"][2], rdot(window[1], local["sz"][:, 0:256])))
 
     def slopes(plane):
         rows = pl.ds(8, BY)

time: 42.8 us -> 42.4 us (level)
  the two profiles are of different devices: /device:TPU:1 before, /device:TPU:8 now
where the time goes in v3:
time: 42.4 us; the launch traced here: 42.3 us
  Pallas kernels  40.3 us (95%)
  local copies, waits for them, and re-layouts  1.36 us (3%)
  between operations  0.64 us (2%)
    pallas_call x1, Pallas kernels, body(): pl.pallas_call(functools.partial(kernel, sizes), out_shape=[jax.ShapeDtyp...  40.3 us
    unnamed x2, local copies, waits for them, and re-layouts  1.36 us

profile of v3, /device:TPU:8, one launch (start us, length us, event | category | flops | bytes accessed | tf_op | source)
XLA Modules:
  0.0 42.3 jit_solution(1587460726901772743)
XLA Ops:
  0.6 40.3 %shard_map.176 = (f32[3,8,16,128]{3,2,1,0:T(8,128)S(1)}, f32[3,8,16,128]{3,2,1,0:T(8,128)S(1)}) custom-call(f32[3,8,16,128]{3,2,1,0:T(8,128)} %lat_hbm.1, f32[3,8,16,128]{3,2,1,0:T(8,128)} %cot_hbm.1, bf16[23,64,720]{2,1,0:T(8,128)(2,1)} %constant.30.clone.refs_0_, bf16[22,64,768]{2,1,0:T(8,128)(2,1)} %constant.31.clone.refs_1_, ...), custom_call_target="tpu_custom_call" | custom-call | tf_op jit(solution)/shard_map/pallas_call | solution.py:657
  40.9 0.7 %copy.21 = f32[3,8,16,128]{3,2,1,0:T(8,128)} copy(f32[3,8,16,128]{3,2,1,0:T(8,128)S(1)} %get-tuple-element.4) | data formatting | bytes 393216
  41.6 0.7 %copy.22 = f32[3,8,16,128]{3,2,1,0:T(8,128)} copy(f32[3,8,16,128]{3,2,1,0:T(8,128)S(1)} %get-tuple-element.5) | data formatting | bytes 393216

commit v4 on v3

--- a/solution.py
+++ b/solution.py
@@ -280,7 +280,7 @@
         t1[0, plane + 3] = spill
         return carry
 
-    lax.fori_loop(0, BX + 2, paint, 0)
+    lax.fori_loop(0, BX + 2, paint, 0, unroll=2)
 
     loads["cd"].wait()
     loads["cq"].wait()
@@ -404,7 +404,7 @@
             f0[q, plane] = f0[q, plane] + jnp.where(edge, pltpu.roll(fixes[q], by, 1), 0.0)
         return carry
 
-    lax.fori_loop(2, BX + 6, fix, 0)
+    lax.fori_loop(2, BX + 6, fix, 0, unroll=2)
     rim_copies = [
         send(f0.at[:, 2:14, 16:24], yrecv.at[0], s_h.at[2], r_h.at[2], "gz", 1),
         send(f0.at[:, 2:14, 0:8], yrecv.at[1], s_h.at[3], r_h.at[3], "gz", ngz - 1),
@@ -485,7 +485,7 @@
             t1[q, plane] = jnp.where(edge, pltpu.roll(rims[q], by, 1), 0.0)
         return carry
 
-    lax.fori_loop(0, WX, unpack, 0)
+    lax.fori_loop(0, WX, unpack, 0, unroll=2)
     window = [
         jnp.concatenate([f0[q].reshape(WX * WY, 128), t1[q].reshape(WX * WY, 128)], axis=1)
         for q in range(2)
@@ -599,7 +599,7 @@
             grad[axis, plane] = (cot[axis, plane] + sums[axis]) * (SMAX * (1.0 - bend * bend))
         return carry
 
-    lax.fori_loop(0, BX, finish, 0)
+    lax.fori_loop(0, BX, finish, 0, unroll=2)
     for copy in started:
         copy.wait_send()
 

time: 42.4 us -> 41 us (0.967)
  the two profiles are of different devices: /device:TPU:8 before, /device:TPU:1 now
where the time goes in v4:
time: 41 us; the launch traced here: 40.2 us
  Pallas kernels  38.3 us (93%)
  local copies, waits for them, and re-layouts  1.36 us (3%)
  between operations  0.64 us (2%)
    pallas_call x1, Pallas kernels, body(): pl.pallas_call(functools.partial(kernel, sizes), out_shape=[jax.ShapeDtyp...  38.3 us
    unnamed x2, local copies, waits for them, and re-layouts  1.36 us

profile of v4, /device:TPU:1, one launch (start us, length us, event | category | flops | bytes accessed | tf_op | source)
XLA Modules:
  0.0 40.2 jit_solution(9322546162897581346)
XLA Ops:
  0.6 38.3 %shard_map.176 = (f32[3,8,16,128]{3,2,1,0:T(8,128)S(1)}, f32[3,8,16,128]{3,2,1,0:T(8,128)S(1)}) custom-call(f32[3,8,16,128]{3,2,1,0:T(8,128)} %lat_hbm.1, f32[3,8,16,128]{3,2,1,0:T(8,128)} %cot_hbm.1, bf16[23,64,720]{2,1,0:T(8,128)(2,1)} %constant.30.clone.refs_0_, bf16[22,64,768]{2,1,0:T(8,128)(2,1)} %constant.31.clone.refs_1_, ...), custom_call_target="tpu_custom_call" | custom-call | tf_op jit(solution)/shard_map/pallas_call | solution.py:657
  38.9 0.7 %copy.21 = f32[3,8,16,128]{3,2,1,0:T(8,128)} copy(f32[3,8,16,128]{3,2,1,0:T(8,128)S(1)} %get-tuple-element.4) | data formatting | bytes 393216
  39.6 0.7 %copy.22 = f32[3,8,16,128]{3,2,1,0:T(8,128)} copy(f32[3,8,16,128]{3,2,1,0:T(8,128)S(1)} %get-tuple-element.5) | data formatting | bytes 393216
